TPU v7x, 32 devices: a whole 2x2x4 slice. The times are simulated.
32 devices in a mesh: dp: 4 (over y, core), ctx: 4 (over z), tp: 2 (over x).
Axes of the slice: x: 2, y: 2, z: 4, core: 2. Of those that a mesh axis runs over, the one named last changes fastest.
Arguments:
- tokens: bfloat16 [8, 1536, 2048], P('dp', ('ctx', 'tp')), may hold values from -6 to 6
- cotangent: bfloat16 [8, 1536, 2048], P('dp', ('ctx', 'tp')), may hold values from -6 to 6
- lengths: int32 [8, 3], P('dp'), may hold values from 129 to 1024, as said below
- head_counts: int32 [2], replicated, may hold values from 8 to 12, as said below
- norm1_gain: float32 [2048], replicated, may hold values from 0.25 to 1.75
- norm2_gain: float32 [2048], replicated, may hold values from 0.25 to 1.75
- q_gain: float32 [64], replicated, may hold values from 0.25 to 1.75
- k_gain: float32 [64], replicated, may hold values from 0.25 to 1.75
- w_query: bfloat16 [2048, 1536], P(('dp', 'ctx'), 'tp'), may hold values from -0.125 to 0.125
- w_key: bfloat16 [2048, 320], replicated, may hold values from -0.125 to 0.125
- w_value: bfloat16 [2048, 320], replicated, may hold values from -0.125 to 0.125
- w_out: bfloat16 [1536, 2048], P('tp', ('dp', 'ctx')), may hold values from -1.25 to 1.25
- w_gate: bfloat16 [2048, 8192], P(('dp', 'ctx'), 'tp'), may hold values from -0.125 to 0.125
- w_up: bfloat16 [2048, 8192], P(('dp', 'ctx'), 'tp'), may hold values from -0.125 to 0.125
- w_down: bfloat16 [8192, 2048], P('tp', ('dp', 'ctx')), may hold values from -0.0625 to 0.0625
Outputs:
- output: bfloat16 [8, 1536, 2048], P('dp', ('ctx', 'tp'))
- d_input: float32 [8, 1536, 2048], P('dp', ('ctx', 'tp'))
- d_norm1: float32 [2048], replicated
- d_norm2: float32 [2048], replicated
- d_qgain: float32 [64], replicated
- d_kgain: float32 [64], replicated
- d_query: float32 [2048, 1536], P(('dp', 'ctx'), 'tp')
- d_key: float32 [2048, 320], replicated
- d_value: float32 [2048, 320], replicated
- d_out: float32 [1536, 2048], P('tp', ('dp', 'ctx'))
- d_gate: float32 [2048, 8192], P(('dp', 'ctx'), 'tp')
- d_up: float32 [2048, 8192], P(('dp', 'ctx'), 'tp')
- d_down: float32 [8192, 2048], P('tp', ('dp', 'ctx'))
Inputs may be any that keep to these rules, and one draw needn't show every extreme that they name: `lengths`: each packed row of 1536 tokens holds three documents: the middle one has 1024 tokens, starts before token 384 and ends after token 1152; the first and the last sum to 512. The counts sum to 20; index t of tp holds the query heads offset_t to offset_t + head_counts[t] - 1, offset_t being the sum over lower indices; some index holds 12.
All inputs are finite; a program needn't handle non-finite values.
Results may differ from a plain program's by a relative error of at most 0.019.
Values may be sent and summed in bfloat16 or wider, within the bound.
No kernel may reach another device: no remote copies, remote signals or barrier semaphores. Data moves between devices by JAX's collectives and lax.ppermute only.
A program may use at most 640 MiB of HBM per device.

v0:
```python
import math
import jax
import jax.numpy as jnp
from jax import lax
from jax.sharding import PartitionSpec as P

HEADS = 20
KVH = 5
HEAD_DIM = 64
EPSILON = 1e-05
THETA = 10000.0
MASKED = -1e30


def rms_norm(value_tensor, gain):
    return (
        value_tensor
        * lax.rsqrt(jnp.mean(value_tensor * value_tensor, axis=-1, keepdims=True) + EPSILON)
        * gain
    )


def rotary(value_tensor, positions):
    half_width = value_tensor.shape[-1] // 2
    indices = jnp.arange(half_width).astype(jnp.float32)
    frequency = jnp.exp(indices * (-2.0 * math.log(THETA) / value_tensor.shape[-1]))
    angles = positions.astype(jnp.float32)[:, None] * frequency[None, :]
    cosine = jnp.cos(angles)[:, None, :]
    sine_of = jnp.sin(angles)[:, None, :]
    first_half = value_tensor[..., :half_width]
    second_half = value_tensor[..., half_width:]
    return jnp.concatenate(
        [first_half * cosine - second_half * sine_of, first_half * sine_of + second_half * cosine],
        axis=-1,
    )


def head_path(projected, gain, positions):
    shaped = projected.reshape(projected.shape[0], projected.shape[1] // HEAD_DIM, HEAD_DIM)
    return rotary(rms_norm(shaped, gain), positions)


def plain_dot(left, right):
    return jnp.dot(left, right, preferred_element_type=jnp.float32)


def dot_last(left, right):
    return lax.dot_general(
        left, right, (((1,), (1,)), ((), ())), preferred_element_type=jnp.float32
    )


def dot_first(left, right):
    return lax.dot_general(
        left, right, (((0,), (0,)), ((), ())), preferred_element_type=jnp.float32
    )


def gather_rows(value_tensor):
    gathered = lax.all_gather(value_tensor, "tp", axis=1, tiled=True)
    return gathered.reshape(gathered.shape[0] * gathered.shape[1], gathered.shape[2])


def sum_rows(term_fn, row_count):
    return lax.psum_scatter(
        term_fn(jnp.int32(0), row_count * lax.axis_size("tp")),
        "tp",
        scatter_dimension=0,
        tiled=True,
    )


def tp_block(value_tensor, count, seq_rows):
    row_total = value_tensor.shape[0]
    width = value_tensor.shape[2]
    span = count // row_total
    block = value_tensor
    block = block.reshape(row_total, span // seq_rows, seq_rows, width)
    return jnp.swapaxes(block, 0, 1).reshape(count, width)


def slot_table(head_counts, slot_count):
    tp_index = lax.axis_index("tp")
    ranks = jnp.arange(head_counts.shape[0])
    offset = jnp.sum(jnp.where(ranks < tp_index, head_counts, 0))
    held = jnp.sum(jnp.where(ranks == tp_index, head_counts, 0))
    slot_ids = jnp.arange(slot_count)
    valid = (slot_ids < held).astype(jnp.float32)
    kv_head = jnp.minimum((offset + slot_ids) // (HEADS // KVH), KVH - 1)
    select = (jnp.arange(KVH)[:, None] == kv_head[None, :]).astype(jnp.bfloat16)
    return (valid, select)


def doc_table(lengths, row_length):
    doc_ends = jnp.cumsum(lengths, axis=1)
    doc_starts = doc_ends - lengths
    token_places = jnp.arange(row_length)[None, :]
    doc_ids = (token_places >= doc_ends[:, 0:1]).astype(jnp.int32) + (
        token_places >= doc_ends[:, 1:2]
    ).astype(jnp.int32)
    begins = jnp.where(
        doc_ids == 0,
        doc_starts[:, 0:1],
        jnp.where(doc_ids == 1, doc_starts[:, 1:2], doc_starts[:, 2:3]),
    )
    return (doc_ids, token_places - begins)


def body(
    tokens,
    cotangent,
    lengths,
    head_counts,
    norm1_gain,
    norm2_gain,
    q_gain,
    k_gain,
    w_query,
    w_key,
    w_value,
    w_out,
    w_gate,
    w_up,
    w_down,
):
    row_total = tokens.shape[0]
    seq_rows = tokens.shape[1]
    stretch_rows = seq_rows * lax.axis_size("tp")
    row_length = stretch_rows * lax.axis_size("ctx")
    local_rows = row_total * seq_rows
    flat_rows = row_total * stretch_rows
    slot_count = w_query.shape[1] // HEAD_DIM
    model_width = w_key.shape[0]
    scale = HEAD_DIM ** (-0.5)
    valid, select = slot_table(head_counts, slot_count)
    doc_ids, positions = doc_table(lengths, row_length)
    own_start = lax.axis_index("ctx") * stretch_rows
    own_docs = lax.dynamic_slice_in_dim(doc_ids, own_start, stretch_rows, 1)
    own_positions = lax.dynamic_slice_in_dim(positions, own_start, stretch_rows, 1).reshape(
        flat_rows
    )
    own_places = own_start + jnp.arange(stretch_rows)
    allowed = (own_docs[:, :, None] == doc_ids[:, None, :]) & (
        own_places[None, :, None] >= jnp.arange(row_length)[None, None, :]
    )
    query_full, out_full, gate_full, up_full, down_full = (
        lax.all_gather(w_query, ("dp", "ctx"), axis=0, tiled=True),
        lax.all_gather(w_out, ("dp", "ctx"), axis=1, tiled=True),
        lax.all_gather(w_gate, ("dp", "ctx"), axis=0, tiled=True),
        lax.all_gather(w_up, ("dp", "ctx"), axis=0, tiled=True),
        lax.all_gather(w_down, ("dp", "ctx"), axis=1, tiled=True),
    )
    key_slots = (
        jnp.einsum(
            "dkh,ks->dsh",
            w_key.reshape(model_width, KVH, HEAD_DIM),
            select,
            preferred_element_type=jnp.float32,
        )
        .astype(jnp.bfloat16)
        .reshape(model_width, slot_count * HEAD_DIM)
    )
    value_slots = (
        jnp.einsum(
            "dkh,ks->dsh",
            w_value.reshape(model_width, KVH, HEAD_DIM),
            select,
            preferred_element_type=jnp.float32,
        )
        .astype(jnp.bfloat16)
        .reshape(model_width, slot_count * HEAD_DIM)
    )

    def by_slot(value_tensor, length):
        return jnp.moveaxis(value_tensor.reshape(row_total, length, slot_count, HEAD_DIM), 2, 1)

    def by_rows(value_tensor, length):
        return jnp.moveaxis(value_tensor, 1, 2).reshape(row_total, length, slot_count * HEAD_DIM)

    def as_rows(value_tensor):
        return value_tensor.reshape(row_total, stretch_rows, value_tensor.shape[-1])

    inputs = tokens.astype(jnp.float32)
    normed_one = gather_rows(rms_norm(inputs, norm1_gain).astype(jnp.bfloat16))
    query_proj = plain_dot(normed_one, query_full)
    key_proj = plain_dot(normed_one, key_slots)
    value_low = plain_dot(normed_one, value_slots).astype(jnp.bfloat16)
    query_low = head_path(query_proj, q_gain, own_positions).astype(jnp.bfloat16)
    key_low = (
        head_path(key_proj, k_gain, own_positions)
        .astype(jnp.bfloat16)
        .reshape(flat_rows, slot_count * HEAD_DIM)
    )
    key_all, value_all = (
        lax.all_gather(as_rows(key_low), "ctx", axis=1, tiled=True),
        lax.all_gather(as_rows(value_low), "ctx", axis=1, tiled=True),
    )
    query_slots = by_slot(query_low, stretch_rows)

    def forward_row(row_pieces):
        row_query, row_keys, row_values, row_allowed = row_pieces

        def forward_slot(pieces):
            query, keys, values = pieces
            scores = jnp.where(row_allowed, dot_last(query, keys) * scale, MASKED)
            peak = jnp.max(scores, axis=1, keepdims=True)
            exp_scores = jnp.exp(scores - peak)
            exp_total = jnp.sum(exp_scores, axis=1, keepdims=True)
            probs_low = (exp_scores / exp_total).astype(jnp.bfloat16)
            return (plain_dot(probs_low, values), (peak + jnp.log(exp_total))[:, 0])

        return lax.map(forward_slot, (row_query, row_keys, row_values))

    attended, log_sums = lax.map(
        forward_row,
        (query_slots, by_slot(key_all, row_length), by_slot(value_all, row_length), allowed),
    )
    out_low = by_rows(attended * valid[None, :, None, None], stretch_rows).astype(jnp.bfloat16)

    def out_term(start, count):
        return plain_dot(tp_block(out_low, count, seq_rows), out_full)

    residual = inputs + sum_rows(out_term, local_rows).reshape(row_total, seq_rows, model_width)
    normed_two = gather_rows(rms_norm(residual, norm2_gain).astype(jnp.bfloat16))
    gate = plain_dot(normed_two, gate_full)
    up_proj = plain_dot(normed_two, up_full)
    sigmoid_gate = jax.nn.sigmoid(gate)
    silu_gate = gate * sigmoid_gate
    hidden = (silu_gate * up_proj).astype(jnp.bfloat16)
    hidden_rows = as_rows(hidden)

    def down_term(start, count):
        return plain_dot(tp_block(hidden_rows, count, seq_rows), down_full)

    output = (
        residual + sum_rows(down_term, local_rows).reshape(row_total, seq_rows, model_width)
    ).astype(jnp.bfloat16)
    grad_out_all = gather_rows(cotangent)
    grad_down = dot_first(hidden, grad_out_all)
    grad_hidden = dot_last(grad_out_all, down_full)
    grad_gate_low = (
        grad_hidden * up_proj * sigmoid_gate * (1.0 + gate * (1.0 - sigmoid_gate))
    ).astype(jnp.bfloat16)
    grad_up_low = (grad_hidden * silu_gate).astype(jnp.bfloat16)
    grad_gate_w = dot_first(normed_two, grad_gate_low)
    grad_up_w = dot_first(normed_two, grad_up_low)
    gate_rows = as_rows(grad_gate_low)
    up_rows = as_rows(grad_up_low)

    def ffn_input_term(start, count):
        return dot_last(tp_block(gate_rows, count, seq_rows), gate_full) + dot_last(
            tp_block(up_rows, count, seq_rows), up_full
        )

    grad_normed_two = sum_rows(ffn_input_term, local_rows).reshape(row_total, seq_rows, model_width)
    _, pull_two = jax.vjp(rms_norm, residual, norm2_gain)
    grad_residual_norm, grad_norm_two = pull_two(grad_normed_two)
    grad_residual = cotangent.astype(jnp.float32) + grad_residual_norm
    grad_attn_all = gather_rows(grad_residual.astype(jnp.bfloat16))
    out_flat = out_low.reshape(flat_rows, slot_count * HEAD_DIM)
    grad_out_w = dot_first(out_flat, grad_attn_all)
    grad_out_low = (
        dot_last(grad_attn_all, out_full) * jnp.repeat(valid, HEAD_DIM)[None, :]
    ).astype(jnp.bfloat16)
    key_back, value_back = (
        lax.all_gather(as_rows(key_low), "ctx", axis=1, tiled=True),
        lax.all_gather(as_rows(value_low), "ctx", axis=1, tiled=True),
    )

    def backward_row(row_pieces):
        row_query, row_keys, row_values, row_sums, row_grads, row_allowed = row_pieces

        def backward_slot(pieces):
            query, keys, values, log_sum, grad_slot = pieces
            scores = jnp.where(row_allowed, dot_last(query, keys) * scale, MASKED)
            probs = jnp.exp(scores - log_sum[:, None])
            grad_probs = dot_last(grad_slot, values)
            inner = jnp.sum(grad_probs * probs, axis=1, keepdims=True)
            grad_scores = (probs * (grad_probs - inner)).astype(jnp.bfloat16)
            grad_query = plain_dot(grad_scores, keys) * scale
            grad_keys = dot_first(grad_scores, query) * scale
            grad_values = dot_first(probs.astype(jnp.bfloat16), grad_slot)
            return (grad_query, grad_keys, grad_values)

        return lax.map(backward_slot, (row_query, row_keys, row_values, row_sums, row_grads))

    grad_query, grad_keys, grad_values = lax.map(
        backward_row,
        (
            query_slots,
            by_slot(key_back, row_length),
            by_slot(value_back, row_length),
            log_sums,
            by_slot(grad_out_low, stretch_rows),
            allowed,
        ),
    )
    grad_key_own, grad_value_own = (
        lax.psum_scatter(
            by_rows(grad_keys, row_length).astype(jnp.bfloat16),
            "ctx",
            scatter_dimension=1,
            tiled=True,
        ).astype(jnp.float32),
        lax.psum_scatter(
            by_rows(grad_values, row_length).astype(jnp.bfloat16),
            "ctx",
            scatter_dimension=1,
            tiled=True,
        ).astype(jnp.float32),
    )
    _, pull_query = jax.vjp(
        lambda projected, gain: head_path(projected, gain, own_positions), query_proj, q_gain
    )
    grad_query_proj, grad_q_gain = pull_query(
        jnp.moveaxis(grad_query, 1, 2).reshape(flat_rows, slot_count, HEAD_DIM)
    )
    _, pull_key = jax.vjp(
        lambda projected, gain: head_path(projected, gain, own_positions), key_proj, k_gain
    )
    grad_key_proj, grad_k_gain = pull_key(grad_key_own.reshape(flat_rows, slot_count, HEAD_DIM))
    grad_query_low = grad_query_proj.astype(jnp.bfloat16)
    grad_key_low = grad_key_proj.astype(jnp.bfloat16)
    grad_value_low = grad_value_own.reshape(flat_rows, slot_count * HEAD_DIM).astype(jnp.bfloat16)
    grad_query_w = dot_first(normed_one, grad_query_low)
    select_float = select.astype(jnp.float32)
    grad_key_w = jnp.einsum(
        "dsh,ks->dkh",
        dot_first(normed_one, grad_key_low).reshape(model_width, slot_count, HEAD_DIM),
        select_float,
        precision=lax.Precision.HIGHEST,
    ).reshape(model_width, KVH * HEAD_DIM)
    grad_value_w = jnp.einsum(
        "dsh,ks->dkh",
        dot_first(normed_one, grad_value_low).reshape(model_width, slot_count, HEAD_DIM),
        select_float,
        precision=lax.Precision.HIGHEST,
    ).reshape(model_width, KVH * HEAD_DIM)
    query_rows = as_rows(grad_query_low)
    key_rows = as_rows(grad_key_low)
    value_rows = as_rows(grad_value_low)

    def attn_input_term(start, count):
        return (
            dot_last(tp_block(query_rows, count, seq_rows), query_full)
            + dot_last(tp_block(key_rows, count, seq_rows), key_slots)
            + dot_last(tp_block(value_rows, count, seq_rows), value_slots)
        )

    grad_normed_one = sum_rows(attn_input_term, local_rows).reshape(
        row_total, seq_rows, model_width
    )
    _, pull_one = jax.vjp(rms_norm, inputs, norm1_gain)
    grad_inputs_norm, grad_norm_one = pull_one(grad_normed_one)
    grad_inputs = grad_residual + grad_inputs_norm
    grad_query_w, grad_out_w, grad_gate_w, grad_up_w, grad_down = (
        lax.psum_scatter(
            grad_query_w.astype(jnp.bfloat16), ("dp", "ctx"), scatter_dimension=0, tiled=True
        ).astype(jnp.float32),
        lax.psum_scatter(
            grad_out_w.astype(jnp.bfloat16), ("dp", "ctx"), scatter_dimension=1, tiled=True
        ).astype(jnp.float32),
        lax.psum_scatter(
            grad_gate_w.astype(jnp.bfloat16), ("dp", "ctx"), scatter_dimension=0, tiled=True
        ).astype(jnp.float32),
        lax.psum_scatter(
            grad_up_w.astype(jnp.bfloat16), ("dp", "ctx"), scatter_dimension=0, tiled=True
        ).astype(jnp.float32),
        lax.psum_scatter(
            grad_down.astype(jnp.bfloat16), ("dp", "ctx"), scatter_dimension=1, tiled=True
        ).astype(jnp.float32),
    )
    grad_key_w, grad_value_w, grad_norm_one, grad_norm_two, grad_q_gain, grad_k_gain = lax.psum(
        (grad_key_w, grad_value_w, grad_norm_one, grad_norm_two, grad_q_gain, grad_k_gain),
        ("dp", "ctx", "tp"),
    )
    return (
        output,
        grad_inputs,
        grad_norm_one,
        grad_norm_two,
        grad_q_gain,
        grad_k_gain,
        grad_query_w,
        grad_key_w,
        grad_value_w,
        grad_out_w,
        grad_gate_w,
        grad_up_w,
        grad_down,
    )


def solution(mesh):
    return jax.shard_map(
        body,
        mesh=mesh,
        in_specs=(
            P("dp", ("ctx", "tp"), None),
            P("dp", ("ctx", "tp"), None),
            P("dp", None),
            P(),
            P(),
            P(),
            P(),
            P(),
            P(("dp", "ctx"), "tp"),
            P(),
            P(),
            P("tp", ("dp", "ctx")),
            P(("dp", "ctx"), "tp"),
            P(("dp", "ctx"), "tp"),
            P("tp", ("dp", "ctx")),
        ),
        out_specs=(
            P("dp", ("ctx", "tp"), None),
            P("dp", ("ctx", "tp"), None),
            P(),
            P(),
            P(),
            P(),
            P(("dp", "ctx"), "tp"),
            P(),
            P(),
            P("tp", ("dp", "ctx")),
            P(("dp", "ctx"), "tp"),
            P(("dp", "ctx"), "tp"),
            P("tp", ("dp", "ctx")),
        ),
        check_vma=False,
    )
```

profile of v0, /device:TPU:0, one launch (start us, length us, event | category | flops | bytes accessed | tf_op | source)
XLA Modules:
  0.0 3367.5 jit_solution(612909178825626275)
XLA Ops:
  20.3 40.3 %all-gather.12.cloned.1.call-done = bf16[2,384,2048]{2,1,0:T(8,128)(2,1)} async-done(((bf16[2,192,2048]{2,1,0:T(8,128)(2,1)}), bf16[2,384,2048]{2,1,0:T(8,128)(2,1)}) %all-gather.12.cloned.1.call-update) | async-done | bytes 3145744 | tf_op jit(solution)/shard_map/all_gather | solution.py:60
  60.5 5.5 convolution_convert_fusion.4
  77.1 30.9 all-gather.14.cloned.1.call-done
  108.1 4.6 copy.95
  112.7 5.7 multiply_reduce_fusion.9
  131.6 5.3 maximum_bitcast_fusion
  136.9 61.6 %all-gather.18.cloned.1.call-done = bf16[2,1536,768]{1,2,0:T(8,128)(2,1)} async-done(((bf16[2,384,768]{1,2,0:T(8,128)(2,1)}), bf16[2,1536,768]{1,2,0:T(8,128)(2,1)}) %all-gather.18.cloned.1.call-update) | async-done | bytes 4718608 | tf_op jit(solution)/shard_map/all_gather | solution.py:196
  198.5 9.7 copy.105
  208.1 80.3 %all-gather.16.cloned.1.call-done = bf16[2,1536,768]{1,2,0:T(8,128)(2,1)} async-done(((bf16[2,384,768]{1,2,0:T(8,128)(2,1)}), bf16[2,1536,768]{1,2,0:T(8,128)(2,1)}) %all-gather.16.cloned.1.call-update) | async-done | bytes 4718608 | tf_op jit(solution)/shard_map/all_gather | solution.py:195
  288.4 9.7 copy.104
  299.8 134.2 %while.53 = (s32[]{:T(128)}, f32[2,12,384,64]{2,3,1,0:T(8,128)}, f32[2,12,384]{2,1,0:T(8,128)S(1)}, bf16[2,12,384,64]{3,2,1,0:T(8,128)(2,1)}, bf16[2,12,1536,64]...) while((s32[]{:T(128)}, f32[2,12,384,64]{2,3,1,0:T(8,128)}, ...), condition=%wide.region_10.11_spmd, body=%wide.region_5.10_spmd.sunk | while | flops 155713152 | bytes 32313720 | solution.py:214
  302.2 8.4 dynamic-slice_bitcast_fusion.18
  310.6 53.8 %while.56 = (s32[]{:T(128)}, f32[12,384,64]{1,2,0:T(8,128)}, f32[12,384]{1,0:T(8,128)S(1)}, bf16[12,384,64]{2,1,0:T(8,128)(2,1)S(1)}, bf16[12,1536,64]{2,1,0:T(8...) while((s32[]{:T(128)}, f32[12,384,64]{1,2,0:T(8,128)}, ...), condition=%wide.region_9.9_spmd, body=%wide.region_6.8_spmd.sunk | while | flops 155713152 | bytes 8671337 | solution.py:212
  369.4 8.4 dynamic-slice_bitcast_fusion.18
  377.7 53.7 %while.56 = (s32[]{:T(128)}, f32[12,384,64]{1,2,0:T(8,128)}, f32[12,384]{1,0:T(8,128)S(1)}, bf16[12,384,64]{2,1,0:T(8,128)(2,1)S(1)}, bf16[12,1536,64]{2,1,0:T(8...) while((s32[]{:T(128)}, f32[12,384,64]{1,2,0:T(8,128)}, ...), condition=%wide.region_9.9_spmd, body=%wide.region_6.8_spmd.sunk | while | flops 155713152 | bytes 8671337 | solution.py:212
  441.8 6.4 fusion.91
  448.3 75.6 %reduce-scatter.20.cloned.1.call-done = f32[384,2048]{1,0:T(8,128)} async-done(((f32[768,2048]{1,0:T(8,128)}), f32[384,2048]{1,0:T(8,128)}) %reduce-scatter.20.cloned.1.call-update) | async-done | bytes 3145744 | tf_op jit(solution)/shard_map/reduce_scatter | solution.py:65
  532.5 42.0 %all-gather.22.cloned.1.call-done = bf16[2,384,2048]{2,1,0:T(8,128)(2,1)} async-done(((bf16[2,192,2048]{2,1,0:T(8,128)(2,1)}), bf16[2,384,2048]{2,1,0:T(8,128)(2,1)}) %all-gather.22.cloned.1.call-update) | async-done | bytes 3145744 | tf_op jit(solution)/shard_map/all_gather | solution.py:60
  574.5 129.4 %all-gather.26.cloned.1.call-done = bf16[2048,4096]{1,0:T(8,128)(2,1)} async-done(((bf16[128,4096]{1,0:T(8,128)(2,1)}), bf16[2048,4096]{1,0:T(8,128)(2,1)}) %all-gather.26.cloned.1.call-update) | async-done | bytes 16777232 | tf_op jit(solution)/shard_map/all_gather | solution.py:150
  703.9 20.2 fusion.93
  724.1 107.4 %all-gather.24.cloned.1.call-done = bf16[2048,4096]{1,0:T(8,128)(2,1)} async-done(((bf16[128,4096]{1,0:T(8,128)(2,1)}), bf16[2048,4096]{1,0:T(8,128)(2,1)}) %all-gather.24.cloned.1.call-update) | async-done | bytes 16777232 | tf_op jit(solution)/shard_map/all_gather | solution.py:149
  831.5 20.2 fusion.92
  851.7 24.4 all-gather.30.cloned.1.call-done
  876.1 132.7 %all-gather.28.cloned.1.call-done = bf16[4096,2048]{1,0:T(8,128)(2,1)} async-done(((bf16[4096,128]{1,0:T(8,128)(2,1)}), bf16[4096,2048]{1,0:T(8,128)(2,1)}) %all-gather.28.cloned.1.call-update) | async-done | bytes 16777232 | tf_op jit(solution)/shard_map/all_gather | solution.py:151
  1008.7 29.0 multiply_convert_fusion.1
  1045.4 18.4 fusion.95
  1063.8 21.3 convolution_add_fusion
  1085.2 75.3 %reduce-scatter.24.cloned.1.call-done = f32[384,2048]{1,0:T(8,128)} async-done(((f32[768,2048]{1,0:T(8,128)}), f32[384,2048]{1,0:T(8,128)}) %reduce-scatter.24.cloned.1.call-update) | async-done | bytes 3145744 | tf_op jit(solution)/shard_map/reduce_scatter | solution.py:65
  1167.7 44.9 %all-gather.32.cloned.1.call-done = bf16[2,384,2048]{2,1,0:T(8,128)(2,1)} async-done(((bf16[2,192,2048]{2,1,0:T(8,128)(2,1)}), bf16[2,384,2048]{2,1,0:T(8,128)(2,1)}) %all-gather.32.cloned.1.call-update) | async-done | bytes 3145744 | tf_op jit(solution)/shard_map/all_gather | solution.py:60
  1212.5 5.5 multiply_convert_fusion.5
  1221.7 258.5 %while.55 = (s32[]{:T(128)}, f32[2,12,384,64]{2,3,1,0:T(8,128)}, bf16[2,12,1536,64]{2,3,1,0:T(8,128)(2,1)}, bf16[2,12,1536,64]{2,3,1,0:T(8,128)(2,1)}, bf16[2,12...) while((s32[]{:T(128)}, f32[2,12,384,64]{2,3,1,0:T(8,128)}, ...), condition=%wide.region_21.22_spmd, body=%wide.region_17.21_spmd.sunk | while | flops 382918272 | bytes 75056560 | solution.py:287
  1229.2 5.2 dynamic-slice_bitcast_fusion.24
  1238.5 105.7 %while.57 = (s32[]{:T(128)}, f32[12,384,64]{1,2,0:T(8,128)}, bf16[12,1536,64]{1,2,0:T(8,128)(2,1)}, bf16[12,1536,64]{1,2,0:T(8,128)(2,1)}, bf16[12,384,64]{2,1,0...) while((s32[]{:T(128)}, f32[12,384,64]{1,2,0:T(8,128)}, ...), condition=%wide.region_20.20_spmd, body=%wide.region_18.19_spmd.sunk | while | flops 382918272 | bytes 20755576 | solution.py:285
  1358.5 5.2 dynamic-slice_bitcast_fusion.24
  1367.8 105.7 %while.57 = (s32[]{:T(128)}, f32[12,384,64]{1,2,0:T(8,128)}, bf16[12,1536,64]{1,2,0:T(8,128)(2,1)}, bf16[12,1536,64]{1,2,0:T(8,128)(2,1)}, bf16[12,384,64]{2,1,0...) while((s32[]{:T(128)}, f32[12,384,64]{1,2,0:T(8,128)}, ...), condition=%wide.region_20.20_spmd, body=%wide.region_18.19_spmd.sunk | while | flops 382918272 | bytes 20755576 | solution.py:285
  1480.2 9.3 copy.116
  1489.5 210.1 %copy.126 = bf16[2,1536,768]{0,2,1:T(8,128)(2,1)} copy(bf16[2,1536,768]{1,0,2:T(2,128)(2,1)} %bitcast.319) | data formatting | bytes 9437184
  1699.6 484.8 %reshape.444 = bf16[1536,1536]{1,0:T(8,128)(2,1)} reshape(bf16[1536,768,2]{2,1,0:T(8,128)(2,1)} %bitcast.94) | data formatting | bytes 9437184
  2184.4 12.6 copy.128
  2197.1 5.5 copy.137
  2209.8 4.7 copy.130
  2214.6 19.7 convolution_convert_fusion
  2234.3 21.4 copy.132
  2255.8 19.8 convolution_convert_fusion.1
  2275.7 20.0 convolution_convert_fusion.2
  2299.2 164.2 %reshape.445 = bf16[384,768,2]{2,1,0:T(8,128)(2,1)} reshape(bf16[384,1536]{1,0:T(8,128)(2,1)} %reduce-scatter.34.cloned.1.call-done) | data formatting | bytes 2359296
  2463.5 68.4 %copy.127 = bf16[2,384,768]{1,0,2:T(2,128)(2,1)S(1)} copy(bf16[2,384,768]{0,2,1:T(8,128)(2,1)} %bitcast.95) | data formatting | bytes 2359296
  2544.4 5.8 convert_element_type.225
  2557.4 4.8 copy.115
  2566.4 4.6 convert_element_type.230
  2572.6 4.6 fusion.97
  2580.0 4.6 add_add_fusion
  2587.9 18.7 fusion.94
  2608.5 4.5 fusion.98
  2613.1 6.5 fusion.53
  2626.6 6.5 fusion.50
  2641.5 149.6 %reduce-scatter.32.cloned.1.call-done = bf16[128,4096]{1,0:T(8,128)(2,1)} async-done(((bf16[2048,4096]{1,0:T(8,128)(2,1)}), bf16[128,4096]{1,0:T(8,128)(2,1)}) %reduce-scatter.32.cloned.1.call-update) | async-done | bytes 1048592 | tf_op jit(solution)/shard_map/reduce_scatter | solution.py:366
  2793.9 179.0 %reduce-scatter.30.cloned.1.call-done = bf16[128,4096]{1,0:T(8,128)(2,1)} async-done(((bf16[2048,4096]{1,0:T(8,128)(2,1)}), bf16[128,4096]{1,0:T(8,128)(2,1)}) %reduce-scatter.30.cloned.1.call-update) | async-done | bytes 1048592 | tf_op jit(solution)/shard_map/reduce_scatter | solution.py:363
  2975.6 66.1 %reduce-scatter.28.cloned.1.call-done = bf16[128,768]{1,0:T(8,128)(2,1)} async-done(((bf16[2048,768]{1,0:T(8,128)(2,1)}), bf16[128,768]{1,0:T(8,128)(2,1)}) %reduce-scatter.28.cloned.1.call-update) | async-done | bytes 196624 | tf_op jit(solution)/shard_map/reduce_scatter | solution.py:357
  3043.4 76.7 %reduce-scatter.26.cloned.1.call-done = f32[384,2048]{1,0:T(8,128)} async-done(((f32[768,2048]{1,0:T(8,128)}), f32[384,2048]{1,0:T(8,128)}) %reduce-scatter.26.cloned.1.call-update) | async-done | bytes 3145744 | tf_op jit(solution)/shard_map/reduce_scatter | solution.py:65
  3123.0 40.2 %all-reduce.4 = (f32[2048]{0:T(1024)}, f32[2048]{0:T(1024)}, f32[64]{0:T(128)}, f32[64]{0:T(128)}) all-reduce(f32[2048]{0:T(1024)S(1)} %get-tuple-element.259, f32[2048]{0:T(1024)S(1)} %copy-done.51, f32[64]{0:T(128)S(1)} %get-tuple-element.257, f32[64]{0:T(128)S(1)} %get-tuple-element.255), channel_id=1, replica_groups=mesh['dp'=4,'ctx'=4,'tp'=2] {'dp','ctx','tp'}, use_global_device_ids=true, to_apply=%region_29.30 | all-reduce | flops 4224 | bytes 33792 | tf_op jit(solution)/shard_map/psum | solution.py:373
  3163.2 37.6 %reduce-scatter.22.cloned.1.call-done = f32[384,2048]{1,0:T(8,128)} async-done(((f32[768,2048]{1,0:T(8,128)}), f32[384,2048]{1,0:T(8,128)}) %reduce-scatter.22.cloned.1.call-update) | async-done | bytes 3145744 | tf_op jit(solution)/shard_map/reduce_scatter | solution.py:65
  3200.8 7.7 fusion.59
  3208.4 146.9 %all-reduce.8.cloned.1.call-done = (f32[2048,320]{0,1:T(8,128)}, f32[2048,320]{0,1:T(8,128)}) async-done(((f32[2048,320]{0,1:T(8,128)}, f32[2048,320]{0,1:T(8,128)}), (f32[2048,320]{0,1:T(8,128)}, f32[2048,320]{0,1:T(8,128)})) %all-reduce.8.cloned.1.call-update) | async-done | bytes 5242896 | tf_op jit(solution)/shard_map/psum | solution.py:373
  (648 shorter events, 512.7 us)
Async XLA Ops:
  7.2 7.6 copy-start
  7.2 53.3 %all-gather.12.cloned.1.call-start = ((), (), s32[]{:S(2)}) async-start(), calls=%async_computation.11 | async-start | bytes 4718592 | tf_op jit(solution)/shard_map/all_gather | solution.py:60
  12.7 95.4 %all-gather.14.cloned.1.call-start = ((), (), s32[]{:S(2)}) async-start(), calls=%async_computation.12 | async-start | bytes 3342336 | tf_op jit(solution)/shard_map/all_gather | solution.py:147
  13.5 185.0 %all-gather.18.cloned.1.call-start = ((), (), s32[]{:S(2)}) async-start(), calls=%async_computation.14 | async-start | bytes 5898240 | tf_op jit(solution)/shard_map/all_gather | solution.py:196
  14.8 54.0 %copy-start.60 = (s32[12]{0:T(128)}, s32[12]{0:T(128)S(1)}, u32[]{:S(2)}) copy-start(s32[12]{0:T(128)S(1)} %fusion.89) | copy-start | bytes 148
  67.5 220.9 %all-gather.16.cloned.1.call-start = ((), (), s32[]{:S(2)}) async-start(), calls=%async_computation.13 | async-start | bytes 5898240 | tf_op jit(solution)/shard_map/all_gather | solution.py:195
  72.6 4.5 copy-start.25
  73.0 46.9 %copy-start.30 = (f32[768,32]{0,1:T(8,128)}, f32[768,32]{0,1:T(8,128)S(1)}, u32[]{:S(2)}) copy-start(f32[768,32]{0,1:T(8,128)S(1)} %get-tuple-element.371) | copy-start | bytes 294916
  73.0 46.9 %copy-start.32 = (f32[768,32]{0,1:T(8,128)}, f32[768,32]{0,1:T(8,128)S(1)}, u32[]{:S(2)}) copy-start(f32[768,32]{0,1:T(8,128)S(1)} %get-tuple-element.372) | copy-start | bytes 294916
  77.1 35.6 %copy-start.40 = (f32[768,12]{0,1:T(8,128)}, f32[768,12]{0,1:T(8,128)S(1)}, u32[]{:S(2)}) copy-start(f32[768,12]{0,1:T(8,128)S(1)} %get-tuple-element.373) | copy-start | bytes 110596
  77.1 41.4 %copy-start.34 = (f32[768,12]{0,1:T(8,128)}, f32[768,12]{0,1:T(8,128)S(1)}, u32[]{:S(2)}) copy-start(f32[768,12]{0,1:T(8,128)S(1)} %fusion.72) | copy-start | bytes 110596
  112.7 5.8 copy-start.13
  112.7 5.8 copy-start.62
  112.7 5.8 copy-start.64
  123.0 3.4 copy-start.28
  123.1 318.7 %all-gather.20.cloned.1.call-start = ((), (), s32[]{:S(2)}) async-start(), calls=%async_computation.15 | async-start | bytes 3342336 | tf_op jit(solution)/shard_map/all_gather | solution.py:148
  123.7 400.2 %reduce-scatter.20.cloned.1.call-start = ((), (), s32[]{:S(2)}) async-start(), calls=%async_computation.16 | async-start | bytes 9437184 | tf_op jit(solution)/shard_map/reduce_scatter | solution.py:65
  299.8 134.2 %copy-start.66 = (f32[12]{0:T(128)S(1)}, f32[12]{0:T(128)}, u32[]{:S(2)}) copy-start(f32[12]{0:T(128)} %compare_convert_fusion.2) | copy-start | bytes 148
  434.0 4.2 copy-start.38
  434.0 14.2 copy-start.8
  448.2 75.7 %copy-start.10 = (bf16[2,192,2048]{2,1,0:T(8,128)(2,1)S(1)}, bf16[2,192,2048]{2,1,0:T(8,128)(2,1)}, u32[]{:S(2)}) copy-start(bf16[2,192,2048]{2,1,0:T(8,128)(2,1)} %param.23) | copy-start | bytes 4718596
  448.2 126.3 %all-gather.22.cloned.1.call-start = ((), (), s32[]{:S(2)}) async-start(), calls=%async_computation.17 | async-start | bytes 4718592 | tf_op jit(solution)/shard_map/all_gather | solution.py:60
  523.9 4.1 copy-start.44
  529.4 174.5 %all-gather.26.cloned.1.call-start = ((), (), s32[]{:S(2)}) async-start(), calls=%async_computation.19 | async-start | bytes 17825792 | tf_op jit(solution)/shard_map/all_gather | solution.py:150
  530.2 301.3 %all-gather.24.cloned.1.call-start = ((), (), s32[]{:S(2)}) async-start(), calls=%async_computation.18 | async-start | bytes 17825792 | tf_op jit(solution)/shard_map/all_gather | solution.py:149
  530.9 345.1 %all-gather.30.cloned.1.call-start = ((), (), s32[]{:S(2)}) async-start(), calls=%async_computation.22 | async-start | bytes 4718592 | tf_op jit(solution)/shard_map/all_gather | solution.py:60
  531.5 477.2 %all-gather.28.cloned.1.call-start = ((), (), s32[]{:S(2)}) async-start(), calls=%async_computation.20 | async-start | bytes 17825792 | tf_op jit(solution)/shard_map/all_gather | solution.py:151
  532.3 628.3 %reduce-scatter.24.cloned.1.call-start = ((), (), s32[]{:S(2)}) async-start(), calls=%async_computation.23 | async-start | bytes 9437184 | tf_op jit(solution)/shard_map/reduce_scatter | solution.py:65
  1037.7 4.0 slice-start
  1037.7 4.7 slice-start.1
  1085.1 75.4 %copy-start.45 = (f32[2048]{0:T(1024)S(1)}, f32[2048]{0:T(1024)}, u32[]{:S(2)}) copy-start(f32[2048]{0:T(1024)} %param.28) | copy-start | bytes 24580
  1085.1 75.4 %copy-start.49 = (f32[2,192]{1,0:T(2,128)S(1)}, f32[2,192]{1,0:T(2,128)}, u32[]{:S(2)}) copy-start(f32[2,192]{1,0:T(2,128)} %copy-done.48) | copy-start | bytes 4612
  1085.1 79.8 %copy-start.17 = (bf16[2,192,2048]{2,1,0:T(8,128)(2,1)S(1)}, bf16[2,192,2048]{2,1,0:T(8,128)(2,1)}, u32[]{:S(2)}) copy-start(bf16[2,192,2048]{2,1,0:T(8,128)(2,1)} %param.24) | copy-start | bytes 4718596
  1085.1 127.4 %all-gather.32.cloned.1.call-start = ((), (), s32[]{:S(2)}) async-start(), calls=%async_computation.24 | async-start | bytes 4718592 | tf_op jit(solution)/shard_map/all_gather | solution.py:60
  1160.5 4.4 copy-start.57
  1160.5 4.4 copy-start.4
  1160.5 4.7 copy-start.12
  1167.4 1131.8 %reduce-scatter.34.cloned.1.call-start = ((), (), s32[]{:S(2)}) async-start(), calls=%async_computation.29 | async-start | bytes 5898240
  1229.2 6.8 copy-start.2
  1358.5 6.8 copy-start.2
  2184.4 365.8 %reduce-scatter.36.cloned.1.call-start = ((), (), s32[]{:S(2)}) async-start(), calls=%async_computation.30 | async-start | bytes 5898240
  2202.6 433.6 %reduce-scatter.38.cloned.1.call-start = ((), (), s32[]{:S(2)}) async-start(), calls=%async_computation.31 | async-start | bytes 3342336
  2214.5 423.5 %reduce-scatter.40.cloned.1.call-start = ((), (), s32[]{:S(2)}) async-start(), calls=%async_computation.32 | async-start | bytes 17825792
  2255.7 535.4 %reduce-scatter.32.cloned.1.call-start = ((), (), s32[]{:S(2)}) async-start(), calls=%async_computation.28 | async-start | bytes 17825792 | tf_op jit(solution)/shard_map/reduce_scatter | solution.py:366
  2275.6 697.2 %reduce-scatter.30.cloned.1.call-start = ((), (), s32[]{:S(2)}) async-start(), calls=%async_computation.27 | async-start | bytes 17825792 | tf_op jit(solution)/shard_map/reduce_scatter | solution.py:363
  2295.8 745.9 %reduce-scatter.28.cloned.1.call-start = ((), (), s32[]{:S(2)}) async-start(), calls=%async_computation.26 | async-start | bytes 3342336 | tf_op jit(solution)/shard_map/reduce_scatter | solution.py:357
  2544.3 575.7 %reduce-scatter.26.cloned.1.call-start = ((), (), s32[]{:S(2)}) async-start(), calls=%async_computation.25 | async-start | bytes 9437184 | tf_op jit(solution)/shard_map/reduce_scatter | solution.py:65
  2556.3 5.9 copy-start.35
  2556.3 5.9 copy-start.65
  2572.6 4.7 copy-start.26
  2572.6 4.7 copy-start.29
  2584.6 616.2 %reduce-scatter.22.cloned.1.call-start = ((), (), s32[]{:S(2)}) async-start(), calls=%async_computation.21 | async-start | bytes 9437184 | tf_op jit(solution)/shard_map/reduce_scatter | solution.py:65
  2606.6 748.7 %all-reduce.8.cloned.1.call-start = ((), (), s32[]{:S(2)}) async-start(), calls=%async_computation.33 | async-start | bytes 10485760 | tf_op jit(solution)/shard_map/psum | solution.py:373
  2608.5 4.6 copy-start.61
  2619.6 4.1 copy-start.73
  2793.9 326.2 %copy-start.11 = (bf16[2,192,2048]{2,1,0:T(8,128)(2,1)S(1)}, bf16[2,192,2048]{2,1,0:T(8,128)(2,1)}, u32[]{:S(2)}) copy-start(bf16[2,192,2048]{2,1,0:T(8,128)(2,1)} %param.23) | copy-start | bytes 4718596
  2793.9 326.2 %copy-start.47 = (f32[2048]{0:T(1024)S(1)}, f32[2048]{0:T(1024)}, u32[]{:S(2)}) copy-start(f32[2048]{0:T(1024)} %param.27) | copy-start | bytes 24580
  2793.9 326.2 %copy-start.53 = (f32[2,192]{1,0:T(2,128)S(1)}, f32[2,192]{1,0:T(2,128)}, u32[]{:S(2)}) copy-start(f32[2,192]{1,0:T(2,128)} %copy-done.52) | copy-start | bytes 4612
  3120.1 43.1 %copy-start.55 = (f32[2,192]{1,0:T(2,128)S(1)}, f32[2,192]{1,0:T(2,128)}, u32[]{:S(2)}) copy-start(f32[2,192]{1,0:T(2,128)} %copy-done.54) | copy-start | bytes 4612
  3120.1 80.7 %copy-start.46 = (f32[2048]{0:T(1024)S(1)}, f32[2048]{0:T(1024)}, u32[]{:S(2)}) copy-start(f32[2048]{0:T(1024)} %param.28) | copy-start | bytes 24580
  3120.1 80.7 %copy-start.50 = (f32[2,192]{1,0:T(2,128)S(1)}, f32[2,192]{1,0:T(2,128)}, u32[]{:S(2)}) copy-start(f32[2,192]{1,0:T(2,128)} %copy-done.48) | copy-start | bytes 4612
  3120.1 80.7 %copy-start.59 = (f32[2,192]{1,0:T(2,128)S(1)}, f32[2,192]{1,0:T(2,128)}, u32[]{:S(2)}) copy-start(f32[2,192]{1,0:T(2,128)} %copy-done.58) | copy-start | bytes 4612
  3355.3 3.7 copy-start.27
  3355.3 5.2 copy-start.1
  (40 other events, 85.4 us)
Sparse Core Ops, SparseCore 0:
  12.8 47.6 all-gather.11
  62.8 45.2 all-gather.13
  110.2 88.1 all-gather.17
  200.5 87.8 all-gather.15
  290.3 46.6 all-gather.19
  448.3 75.5 reduce-scatter.19
  529.6 44.9 all-gather.21
  577.0 126.8 all-gather.25
  706.4 125.0 all-gather.23
  832.9 43.0 all-gather.29
  878.4 130.3 all-gather.27
  1085.3 75.2 reduce-scatter.23
  1167.6 44.9 all-gather.31
  2184.5 85.2 reduce-scatter.33
  2272.0 85.7 reduce-scatter.35
  2361.4 66.7 reduce-scatter.37
  2432.2 177.4 reduce-scatter.39
  2613.6 177.4 reduce-scatter.31
  2795.2 177.5 reduce-scatter.29
  2976.5 65.1 reduce-scatter.27
  3044.0 76.0 reduce-scatter.25
  3122.5 78.2 reduce-scatter.21
  3207.7 147.5 all-reduce.7
where the time goes:
time: 3390 us; the launch traced here: 3370 us
  waiting for transfers between devices  1500 us (44%)
  local copies, waits for them, and re-layouts  1170 us (35%)
  matrix products  557 us (16%)
  other arithmetic  78.4 us (2%)
  blocking collectives  40.2 us (1%)
    unnamed x159, local copies, waits for them, and re-layouts  995 us
    reduce_scatter x4, waiting for transfers between devices, sum_rows(): lax.psum_scatter(term_fn(jnp.int32(0), row_count * lax.axis_size('tp')),...  265 us
    dot_general x79, matrix products, dot_last(): lax.dot_general(left, right, (((1,), (1,)), ((), ())), preferred_element_...  205 us
    dot_general x55, matrix products, plain_dot(): return jnp.dot(left, right, preferred_element_type=jnp.float32)  188 us
    reduce_scatter x1, waiting for transfers between devices, body(): lax.psum_scatter(grad_gate_w.astype(jnp.bfloat16), ('dp', 'ctx'), scatter...  179 us
    all_gather x4, waiting for transfers between devices, gather_rows(): gathered = lax.all_gather(value_tensor, 'tp', axis=1, tiled=True)  152 us
    reduce_scatter x1, waiting for transfers between devices, body(): lax.psum_scatter(grad_up_w.astype(jnp.bfloat16), ('dp', 'ctx'), scatter_d...  150 us
    dot_general x55, matrix products, dot_first(): lax.dot_general(left, right, (((0,), (0,)), ((), ())), preferred_element_...  147 us
  transfers between devices with their start and end apart: 23, of which 18 were waited for; matrix products, arithmetic and copies ran while one was open for 21% of the time, Pallas kernels for 0%

commit v1 on v0

--- a/solution.py
+++ b/solution.py
@@ -1,3 +1,4 @@
+import functools
 import math
 import jax
 import jax.numpy as jnp
@@ -10,6 +11,15 @@
 EPSILON = 1e-05
 THETA = 10000.0
 MASKED = -1e30
+
+
+def save_the_islands(a0, mesh_dim, row_axis):
+    for t in (mesh_dim, row_axis):
+        a0 = jax.lax.psum(a0, t)
+    return a0
+
+
+reach_the_threads = functools.partial(save_the_islands, mesh_dim=("ctx", "tp"), row_axis="dp")
 
 
 def rms_norm(value_tensor, gain):
@@ -370,9 +380,10 @@
             grad_down.astype(jnp.bfloat16), ("dp", "ctx"), scatter_dimension=1, tiled=True
         ).astype(jnp.float32),
     )
-    grad_key_w, grad_value_w, grad_norm_one, grad_norm_two, grad_q_gain, grad_k_gain = lax.psum(
-        (grad_key_w, grad_value_w, grad_norm_one, grad_norm_two, grad_q_gain, grad_k_gain),
-        ("dp", "ctx", "tp"),
+    grad_key_w, grad_value_w, grad_norm_one, grad_norm_two, grad_q_gain, grad_k_gain = (
+        reach_the_threads(
+            (grad_key_w, grad_value_w, grad_norm_one, grad_norm_two, grad_q_gain, grad_k_gain)
+        )
     )
     return (
         output,

time: 3390 us -> 3710 us (1.094)
  waiting for transfers between devices: 1500 us -> 1820 us
    unnamed x27 -> x28, waiting for transfers between devices: 4.13 us -> 317 us
    psum x1 -> x2, waiting for transfers between devices: 147 us -> 129 us  [save_the_islands(): a0 = jax.lax.psum(a0, t)]
  transfers between devices with their start and end apart: 23 -> 24, of which waited for: 18 -> 22; matrix products, arithmetic and copies ran while one was open for 21% -> 31% of each run, Pallas kernels for 0% -> 0%
where the time goes in v1:
time: 3710 us; the launch traced here: 3680 us
  waiting for transfers between devices  1820 us (49%)
  local copies, waits for them, and re-layouts  1160 us (31%)
  matrix products  557 us (15%)
  other arithmetic  77.5 us (2%)
  blocking collectives  48.6 us (1%)
    unnamed x159, local copies, waits for them, and re-layouts  991 us
    unnamed x28, waiting for transfers between devices  317 us
    reduce_scatter x4, waiting for transfers between devices, sum_rows(): lax.psum_scatter(term_fn(jnp.int32(0), row_count * lax.axis_size('tp')),...  257 us
    dot_general x79, matrix products, dot_last(): lax.dot_general(left, right, (((1,), (1,)), ((), ())), preferred_element_...  205 us
    dot_general x55, matrix products, plain_dot(): return jnp.dot(left, right, preferred_element_type=jnp.float32)  188 us
    reduce_scatter x1, waiting for transfers between devices, body(): lax.psum_scatter(grad_gate_w.astype(jnp.bfloat16), ('dp', 'ctx'), scatter...  179 us
    reduce_scatter x1, waiting for transfers between devices, body(): lax.psum_scatter(grad_up_w.astype(jnp.bfloat16), ('dp', 'ctx'), scatter_d...  179 us
    all_gather x4, waiting for transfers between devices, gather_rows(): gathered = lax.all_gather(value_tensor, 'tp', axis=1, tiled=True)  151 us
  transfers between devices with their start and end apart: 24, of which 22 were waited for; matrix products, arithmetic and copies ran while one was open for 31% of the time, Pallas kernels for 0%

profile of v1, /device:TPU:0, one launch (start us, length us, event | category | flops | bytes accessed | tf_op | source)
XLA Modules:
  0.0 3684.1 jit_solution(2703816156928916872)
XLA Ops:
  20.2 40.3 %all-gather.12.cloned.1.call-done = bf16[2,384,2048]{2,1,0:T(8,128)(2,1)} async-done(((bf16[2,192,2048]{2,1,0:T(8,128)(2,1)}), bf16[2,384,2048]{2,1,0:T(8,128)(2,1)}) %all-gather.12.cloned.1.call-update) | async-done | bytes 3145744 | tf_op jit(solution)/shard_map/all_gather | solution.py:70
  60.5 5.5 convolution_convert_fusion.4
  76.8 31.2 all-gather.14.cloned.1.call-done
  112.7 5.7 multiply_reduce_fusion.9
  131.5 5.1 maximum_bitcast_fusion
  136.6 61.8 %all-gather.18.cloned.1.call-done = bf16[2,1536,768]{1,2,0:T(8,128)(2,1)} async-done(((bf16[2,384,768]{1,2,0:T(8,128)(2,1)}), bf16[2,1536,768]{1,2,0:T(8,128)(2,1)}) %all-gather.18.cloned.1.call-update) | async-done | bytes 4718608 | tf_op jit(solution)/shard_map/all_gather | solution.py:206
  198.4 9.7 copy.105
  208.1 80.3 %all-gather.16.cloned.1.call-done = bf16[2,1536,768]{1,2,0:T(8,128)(2,1)} async-done(((bf16[2,384,768]{1,2,0:T(8,128)(2,1)}), bf16[2,1536,768]{1,2,0:T(8,128)(2,1)}) %all-gather.16.cloned.1.call-update) | async-done | bytes 4718608 | tf_op jit(solution)/shard_map/all_gather | solution.py:205
  288.3 9.7 copy.104
  299.7 134.2 %while.53 = (s32[]{:T(128)}, f32[2,12,384,64]{2,3,1,0:T(8,128)}, f32[2,12,384]{2,1,0:T(8,128)S(1)}, bf16[2,12,384,64]{3,2,1,0:T(8,128)(2,1)}, bf16[2,12,1536,64]...) while((s32[]{:T(128)}, f32[2,12,384,64]{2,3,1,0:T(8,128)}, ...), condition=%wide.region_10.11_spmd, body=%wide.region_5.10_spmd.sunk | while | flops 155713152 | bytes 32313720 | solution.py:224
  302.1 8.4 dynamic-slice_bitcast_fusion.18
  310.5 53.8 %while.56 = (s32[]{:T(128)}, f32[12,384,64]{1,2,0:T(8,128)}, f32[12,384]{1,0:T(8,128)S(1)}, bf16[12,384,64]{2,1,0:T(8,128)(2,1)S(1)}, bf16[12,1536,64]{2,1,0:T(8...) while((s32[]{:T(128)}, f32[12,384,64]{1,2,0:T(8,128)}, ...), condition=%wide.region_9.9_spmd, body=%wide.region_6.8_spmd.sunk | while | flops 155713152 | bytes 8671337 | solution.py:222
  369.4 8.4 dynamic-slice_bitcast_fusion.18
  377.7 53.7 %while.56 = (s32[]{:T(128)}, f32[12,384,64]{1,2,0:T(8,128)}, f32[12,384]{1,0:T(8,128)S(1)}, bf16[12,384,64]{2,1,0:T(8,128)(2,1)S(1)}, bf16[12,1536,64]{2,1,0:T(8...) while((s32[]{:T(128)}, f32[12,384,64]{1,2,0:T(8,128)}, ...), condition=%wide.region_9.9_spmd, body=%wide.region_6.8_spmd.sunk | while | flops 155713152 | bytes 8671337 | solution.py:222
  441.8 6.4 fusion.91
  448.2 75.6 %reduce-scatter.20.cloned.1.call-done = f32[384,2048]{1,0:T(8,128)} async-done(((f32[768,2048]{1,0:T(8,128)}), f32[384,2048]{1,0:T(8,128)}) %reduce-scatter.20.cloned.1.call-update) | async-done | bytes 3145744 | tf_op jit(solution)/shard_map/reduce_scatter | solution.py:75
  532.6 41.8 %all-gather.22.cloned.1.call-done = bf16[2,384,2048]{2,1,0:T(8,128)(2,1)} async-done(((bf16[2,192,2048]{2,1,0:T(8,128)(2,1)}), bf16[2,384,2048]{2,1,0:T(8,128)(2,1)}) %all-gather.22.cloned.1.call-update) | async-done | bytes 3145744 | tf_op jit(solution)/shard_map/all_gather | solution.py:70
  574.4 129.4 %all-gather.26.cloned.1.call-done = bf16[2048,4096]{1,0:T(8,128)(2,1)} async-done(((bf16[128,4096]{1,0:T(8,128)(2,1)}), bf16[2048,4096]{1,0:T(8,128)(2,1)}) %all-gather.26.cloned.1.call-update) | async-done | bytes 16777232 | tf_op jit(solution)/shard_map/all_gather | solution.py:160
  703.8 20.2 fusion.93
  724.0 107.3 %all-gather.24.cloned.1.call-done = bf16[2048,4096]{1,0:T(8,128)(2,1)} async-done(((bf16[128,4096]{1,0:T(8,128)(2,1)}), bf16[2048,4096]{1,0:T(8,128)(2,1)}) %all-gather.24.cloned.1.call-update) | async-done | bytes 16777232 | tf_op jit(solution)/shard_map/all_gather | solution.py:159
  831.3 20.2 fusion.92
  851.5 24.4 all-gather.30.cloned.1.call-done
  875.9 132.7 %all-gather.28.cloned.1.call-done = bf16[4096,2048]{1,0:T(8,128)(2,1)} async-done(((bf16[4096,128]{1,0:T(8,128)(2,1)}), bf16[4096,2048]{1,0:T(8,128)(2,1)}) %all-gather.28.cloned.1.call-update) | async-done | bytes 16777232 | tf_op jit(solution)/shard_map/all_gather | solution.py:161
  1008.6 28.8 multiply_convert_fusion.1
  1045.1 18.4 fusion.95
  1063.5 21.5 convolution_add_fusion
  1085.1 75.3 %reduce-scatter.24.cloned.1.call-done = f32[384,2048]{1,0:T(8,128)} async-done(((f32[768,2048]{1,0:T(8,128)}), f32[384,2048]{1,0:T(8,128)}) %reduce-scatter.24.cloned.1.call-update) | async-done | bytes 3145744 | tf_op jit(solution)/shard_map/reduce_scatter | solution.py:75
  1167.5 44.9 %all-gather.32.cloned.1.call-done = bf16[2,384,2048]{2,1,0:T(8,128)(2,1)} async-done(((bf16[2,192,2048]{2,1,0:T(8,128)(2,1)}), bf16[2,384,2048]{2,1,0:T(8,128)(2,1)}) %all-gather.32.cloned.1.call-update) | async-done | bytes 3145744 | tf_op jit(solution)/shard_map/all_gather | solution.py:70
  1212.4 5.5 multiply_convert_fusion.5
  1221.5 258.5 %while.55 = (s32[]{:T(128)}, f32[2,12,384,64]{2,3,1,0:T(8,128)}, bf16[2,12,1536,64]{2,3,1,0:T(8,128)(2,1)}, bf16[2,12,1536,64]{2,3,1,0:T(8,128)(2,1)}, bf16[2,12...) while((s32[]{:T(128)}, f32[2,12,384,64]{2,3,1,0:T(8,128)}, ...), condition=%wide.region_21.22_spmd, body=%wide.region_17.21_spmd.sunk | while | flops 382918272 | bytes 75056560 | solution.py:297
  1229.0 5.2 dynamic-slice_bitcast_fusion.24
  1238.3 105.7 %while.57 = (s32[]{:T(128)}, f32[12,384,64]{1,2,0:T(8,128)}, bf16[12,1536,64]{1,2,0:T(8,128)(2,1)}, bf16[12,1536,64]{1,2,0:T(8,128)(2,1)}, bf16[12,384,64]{2,1,0...) while((s32[]{:T(128)}, f32[12,384,64]{1,2,0:T(8,128)}, ...), condition=%wide.region_20.20_spmd, body=%wide.region_18.19_spmd.sunk | while | flops 382918272 | bytes 20755576 | solution.py:295
  1358.2 5.2 dynamic-slice_bitcast_fusion.24
  1367.5 105.7 %while.57 = (s32[]{:T(128)}, f32[12,384,64]{1,2,0:T(8,128)}, bf16[12,1536,64]{1,2,0:T(8,128)(2,1)}, bf16[12,1536,64]{1,2,0:T(8,128)(2,1)}, bf16[12,384,64]{2,1,0...) while((s32[]{:T(128)}, f32[12,384,64]{1,2,0:T(8,128)}, ...), condition=%wide.region_20.20_spmd, body=%wide.region_18.19_spmd.sunk | while | flops 382918272 | bytes 20755576 | solution.py:295
  1480.0 12.5 copy.128
  1492.5 5.4 copy.137
  1498.0 9.3 copy.116
  1507.3 210.1 %copy.126 = bf16[2,1536,768]{0,2,1:T(8,128)(2,1)} copy(bf16[2,1536,768]{1,0,2:T(2,128)(2,1)} %bitcast.319) | data formatting | bytes 9437184
  1717.3 484.4 %reshape.444 = bf16[1536,1536]{1,0:T(8,128)(2,1)} reshape(bf16[1536,768,2]{2,1,0:T(8,128)(2,1)} %bitcast.94) | data formatting | bytes 9437184
  2213.8 6.5 fusion.53
  2223.3 63.9 %reduce-scatter.34.cloned.1.call-done = bf16[384,1536]{1,0:T(8,128)(2,1)} async-done(((bf16[1536,1536]{1,0:T(8,128)(2,1)}), bf16[384,1536]{1,0:T(8,128)(2,1)}) %reduce-scatter.34.cloned.1.call-update) | async-done | bytes 1179664
  2287.2 164.0 %reshape.445 = bf16[384,768,2]{2,1,0:T(8,128)(2,1)} reshape(bf16[384,1536]{1,0:T(8,128)(2,1)} %reduce-scatter.34.cloned.1.call-done) | data formatting | bytes 2359296
  2451.2 67.8 %copy.127 = bf16[2,384,768]{1,0,2:T(2,128)(2,1)S(1)} copy(bf16[2,384,768]{0,2,1:T(8,128)(2,1)} %bitcast.95) | data formatting | bytes 2359296
  2530.5 6.5 fusion.50
  2552.2 19.6 convolution_convert_fusion
  2571.9 20.8 copy.132
  2592.7 20.1 convolution_convert_fusion.1
  2612.9 19.8 convolution_convert_fusion.2
  2642.5 5.7 convert_element_type.225
  2654.0 4.8 copy.117
  2658.8 5.0 fusion.97
  2674.4 18.7 fusion.94
  2693.2 32.1 all-reduce.11.cloned.1.call-done
  2725.3 68.9 %reduce-scatter.38.cloned.1.call-done = bf16[128,768]{1,0:T(8,128)(2,1)} async-done(((bf16[2048,768]{1,0:T(8,128)(2,1)}), bf16[128,768]{1,0:T(8,128)(2,1)}) %reduce-scatter.38.cloned.1.call-update) | async-done | bytes 196624
  2796.0 179.6 %reduce-scatter.40.cloned.1.call-done = bf16[128,4096]{1,0:T(8,128)(2,1)} async-done(((bf16[2048,4096]{1,0:T(8,128)(2,1)}), bf16[128,4096]{1,0:T(8,128)(2,1)}) %reduce-scatter.40.cloned.1.call-update) | async-done | bytes 1048592
  2978.7 178.6 %reduce-scatter.32.cloned.1.call-done = bf16[128,4096]{1,0:T(8,128)(2,1)} async-done(((bf16[2048,4096]{1,0:T(8,128)(2,1)}), bf16[128,4096]{1,0:T(8,128)(2,1)}) %reduce-scatter.32.cloned.1.call-update) | async-done | bytes 1048592 | tf_op jit(solution)/shard_map/reduce_scatter | solution.py:376
  3160.1 178.8 %reduce-scatter.30.cloned.1.call-done = bf16[128,4096]{1,0:T(8,128)(2,1)} async-done(((bf16[2048,4096]{1,0:T(8,128)(2,1)}), bf16[128,4096]{1,0:T(8,128)(2,1)}) %reduce-scatter.30.cloned.1.call-update) | async-done | bytes 1048592 | tf_op jit(solution)/shard_map/reduce_scatter | solution.py:373
  3341.6 66.3 %reduce-scatter.28.cloned.1.call-done = bf16[128,768]{1,0:T(8,128)(2,1)} async-done(((bf16[2048,768]{1,0:T(8,128)(2,1)}), bf16[128,768]{1,0:T(8,128)(2,1)}) %reduce-scatter.28.cloned.1.call-update) | async-done | bytes 196624 | tf_op jit(solution)/shard_map/reduce_scatter | solution.py:367
  3409.6 76.6 %reduce-scatter.26.cloned.1.call-done = f32[384,2048]{1,0:T(8,128)} async-done(((f32[768,2048]{1,0:T(8,128)}), f32[384,2048]{1,0:T(8,128)}) %reduce-scatter.26.cloned.1.call-update) | async-done | bytes 3145744 | tf_op jit(solution)/shard_map/reduce_scatter | solution.py:75
  3489.1 37.0 %all-reduce.4 = (f32[2048]{0:T(1024)S(1)}, f32[2048]{0:T(1024)S(1)}, f32[64]{0:T(128)S(1)}, f32[64]{0:T(128)S(1)}) all-reduce(f32[2048]{0:T(1024)S(1)} %get-tuple-element.259, f32[2048]{0:T(1024)S(1)} %copy-done.50, f32[64]{0:T(128)S(1)} %get-tuple-element.257, f32[64]{0:T(128)S(1)} %copy-done.69), channel_id=1, replica_groups=mesh['dp'=4,'ctx'=4,'tp'=2] {'ctx','tp'}, use_global_device_ids=true, to_apply=%region_29.30 | all-reduce | flops 4224 | bytes 33792 | tf_op jit(solution)/shard_map/psum | solution.py:18
  3526.1 11.6 all-reduce.6
  3537.8 29.1 reduce-scatter.22.cloned.1.call-done
  3566.8 7.7 fusion.59
  3574.5 97.3 %all-reduce.13.cloned.1.call-done = (f32[2048,320]{0,1:T(8,128)}, f32[2048,320]{0,1:T(8,128)}) async-done(((f32[2048,320]{0,1:T(8,128)}, f32[2048,320]{0,1:T(8,128)}), (f32[2048,320]{0,1:T(8,128)}, f32[2048,320]{0,1:T(8,128)})) %all-reduce.13.cloned.1.call-update) | async-done | bytes 5242896 | tf_op jit(solution)/shard_map/psum | solution.py:18
  (652 shorter events, 530.3 us)
Async XLA Ops:
  7.2 7.6 copy-start
  7.2 53.3 %all-gather.12.cloned.1.call-start = ((), (), s32[]{:S(2)}) async-start(), calls=%async_computation.11 | async-start | bytes 4718592 | tf_op jit(solution)/shard_map/all_gather | solution.py:70
  12.7 95.3 %all-gather.14.cloned.1.call-start = ((), (), s32[]{:S(2)}) async-start(), calls=%async_computation.12 | async-start | bytes 3342336 | tf_op jit(solution)/shard_map/all_gather | solution.py:157
  13.4 185.0 %all-gather.18.cloned.1.call-start = ((), (), s32[]{:S(2)}) async-start(), calls=%async_computation.14 | async-start | bytes 5898240 | tf_op jit(solution)/shard_map/all_gather | solution.py:206
  14.8 53.6 %copy-start.59 = (s32[12]{0:T(128)}, s32[12]{0:T(128)S(1)}, u32[]{:S(2)}) copy-start(s32[12]{0:T(128)S(1)} %fusion.89) | copy-start | bytes 148
  67.4 220.9 %all-gather.16.cloned.1.call-start = ((), (), s32[]{:S(2)}) async-start(), calls=%async_computation.13 | async-start | bytes 5898240 | tf_op jit(solution)/shard_map/all_gather | solution.py:205
  72.2 4.6 copy-start.25
  72.6 47.2 %copy-start.29 = (f32[768,32]{0,1:T(8,128)}, f32[768,32]{0,1:T(8,128)S(1)}, u32[]{:S(2)}) copy-start(f32[768,32]{0,1:T(8,128)S(1)} %get-tuple-element.377) | copy-start | bytes 294916
  72.6 47.2 %copy-start.31 = (f32[768,32]{0,1:T(8,128)}, f32[768,32]{0,1:T(8,128)S(1)}, u32[]{:S(2)}) copy-start(f32[768,32]{0,1:T(8,128)S(1)} %get-tuple-element.378) | copy-start | bytes 294916
  76.8 35.9 copy-start.41
  76.8 41.7 %copy-start.35 = (f32[768,12]{0,1:T(8,128)}, f32[768,12]{0,1:T(8,128)S(1)}, u32[]{:S(2)}) copy-start(f32[768,12]{0,1:T(8,128)S(1)} %fusion.72) | copy-start | bytes 110596
  112.6 5.8 copy-start.15
  112.6 5.8 copy-start.61
  112.6 5.8 copy-start.63
  123.0 3.3 copy-start.28
  123.0 318.7 %all-gather.20.cloned.1.call-start = ((), (), s32[]{:S(2)}) async-start(), calls=%async_computation.15 | async-start | bytes 3342336 | tf_op jit(solution)/shard_map/all_gather | solution.py:158
  123.6 400.2 %reduce-scatter.20.cloned.1.call-start = ((), (), s32[]{:S(2)}) async-start(), calls=%async_computation.16 | async-start | bytes 9437184 | tf_op jit(solution)/shard_map/reduce_scatter | solution.py:75
  299.7 134.3 %copy-start.65 = (f32[12]{0:T(128)S(1)}, f32[12]{0:T(128)}, u32[]{:S(2)}) copy-start(f32[12]{0:T(128)} %compare_convert_fusion.2) | copy-start | bytes 148
  434.0 4.2 copy-start.37
  434.0 14.2 copy-start.8
  448.1 75.7 %copy-start.10 = (bf16[2,192,2048]{2,1,0:T(8,128)(2,1)S(1)}, bf16[2,192,2048]{2,1,0:T(8,128)(2,1)}, u32[]{:S(2)}) copy-start(bf16[2,192,2048]{2,1,0:T(8,128)(2,1)} %param.23) | copy-start | bytes 4718596
  448.2 126.3 %all-gather.22.cloned.1.call-start = ((), (), s32[]{:S(2)}) async-start(), calls=%async_computation.17 | async-start | bytes 4718592 | tf_op jit(solution)/shard_map/all_gather | solution.py:70
  523.8 4.1 copy-start.43
  529.4 174.5 %all-gather.26.cloned.1.call-start = ((), (), s32[]{:S(2)}) async-start(), calls=%async_computation.19 | async-start | bytes 17825792 | tf_op jit(solution)/shard_map/all_gather | solution.py:160
  530.1 301.2 %all-gather.24.cloned.1.call-start = ((), (), s32[]{:S(2)}) async-start(), calls=%async_computation.18 | async-start | bytes 17825792 | tf_op jit(solution)/shard_map/all_gather | solution.py:159
  530.9 345.1 %all-gather.30.cloned.1.call-start = ((), (), s32[]{:S(2)}) async-start(), calls=%async_computation.22 | async-start | bytes 4718592 | tf_op jit(solution)/shard_map/all_gather | solution.py:70
  531.4 477.1 %all-gather.28.cloned.1.call-start = ((), (), s32[]{:S(2)}) async-start(), calls=%async_computation.20 | async-start | bytes 17825792 | tf_op jit(solution)/shard_map/all_gather | solution.py:161
  532.2 628.2 %reduce-scatter.24.cloned.1.call-start = ((), (), s32[]{:S(2)}) async-start(), calls=%async_computation.23 | async-start | bytes 9437184 | tf_op jit(solution)/shard_map/reduce_scatter | solution.py:75
  1037.3 4.0 slice-start
  1037.3 4.7 slice-start.1
  1085.0 75.4 %copy-start.44 = (f32[2048]{0:T(1024)S(1)}, f32[2048]{0:T(1024)}, u32[]{:S(2)}) copy-start(f32[2048]{0:T(1024)} %param.28) | copy-start | bytes 24580
  1085.0 75.4 %copy-start.48 = (f32[2,192]{1,0:T(2,128)S(1)}, f32[2,192]{1,0:T(2,128)}, u32[]{:S(2)}) copy-start(f32[2,192]{1,0:T(2,128)} %copy-done.47) | copy-start | bytes 4612
  1085.0 79.8 %copy-start.17 = (bf16[2,192,2048]{2,1,0:T(8,128)(2,1)S(1)}, bf16[2,192,2048]{2,1,0:T(8,128)(2,1)}, u32[]{:S(2)}) copy-start(bf16[2,192,2048]{2,1,0:T(8,128)(2,1)} %param.24) | copy-start | bytes 4718596
  1085.0 127.4 %all-gather.32.cloned.1.call-start = ((), (), s32[]{:S(2)}) async-start(), calls=%async_computation.24 | async-start | bytes 4718592 | tf_op jit(solution)/shard_map/all_gather | solution.py:70
  1160.4 4.4 copy-start.56
  1160.4 4.4 copy-start.4
  1160.4 4.7 copy-start.12
  1167.3 1037.8 %reduce-scatter.36.cloned.1.call-start = ((), (), s32[]{:S(2)}) async-start(), calls=%async_computation.30 | async-start | bytes 5898240
  1229.0 6.8 copy-start.2
  1358.2 6.8 copy-start.2
  1497.9 789.3 %reduce-scatter.34.cloned.1.call-start = ((), (), s32[]{:S(2)}) async-start(), calls=%async_computation.29 | async-start | bytes 5898240
  2201.8 523.5 %all-reduce.11.cloned.1.call-start = ((), (), s32[]{:S(2)}) async-start(), calls=%async_computation.33 | async-start | bytes 10485760 | tf_op jit(solution)/shard_map/psum | solution.py:18
  2208.2 5.6 copy-start.19
  2209.2 4.5 copy-start.60
  2540.3 253.9 %reduce-scatter.38.cloned.1.call-start = ((), (), s32[]{:S(2)}) async-start(), calls=%async_computation.31 | async-start | bytes 3342336
  2552.2 423.5 %reduce-scatter.40.cloned.1.call-start = ((), (), s32[]{:S(2)}) async-start(), calls=%async_computation.32 | async-start | bytes 17825792
  2592.6 564.7 %reduce-scatter.32.cloned.1.call-start = ((), (), s32[]{:S(2)}) async-start(), calls=%async_computation.28 | async-start | bytes 17825792 | tf_op jit(solution)/shard_map/reduce_scatter | solution.py:376
  2612.8 726.0 %reduce-scatter.30.cloned.1.call-start = ((), (), s32[]{:S(2)}) async-start(), calls=%async_computation.27 | async-start | bytes 17825792 | tf_op jit(solution)/shard_map/reduce_scatter | solution.py:373
  2632.6 775.3 %reduce-scatter.28.cloned.1.call-start = ((), (), s32[]{:S(2)}) async-start(), calls=%async_computation.26 | async-start | bytes 3342336 | tf_op jit(solution)/shard_map/reduce_scatter | solution.py:367
  2642.4 5.8 copy-start.22
  2642.4 7.9 copy-start.20
  2642.4 843.8 %reduce-scatter.26.cloned.1.call-start = ((), (), s32[]{:S(2)}) async-start(), calls=%async_computation.25 | async-start | bytes 9437184 | tf_op jit(solution)/shard_map/reduce_scatter | solution.py:75
  2658.8 5.0 copy-start.26
  2671.1 895.7 %reduce-scatter.22.cloned.1.call-start = ((), (), s32[]{:S(2)}) async-start(), calls=%async_computation.21 | async-start | bytes 9437184 | tf_op jit(solution)/shard_map/reduce_scatter | solution.py:75
  2693.1 978.7 %all-reduce.13.cloned.1.call-start = ((), (), s32[]{:S(2)}) async-start(), calls=%async_computation.34 | async-start | bytes 10485760 | tf_op jit(solution)/shard_map/psum | solution.py:18
  3160.1 326.1 %copy-start.11 = (bf16[2,192,2048]{2,1,0:T(8,128)(2,1)S(1)}, bf16[2,192,2048]{2,1,0:T(8,128)(2,1)}, u32[]{:S(2)}) copy-start(bf16[2,192,2048]{2,1,0:T(8,128)(2,1)} %param.23) | copy-start | bytes 4718596
  3160.1 326.1 %copy-start.46 = (f32[2048]{0:T(1024)S(1)}, f32[2048]{0:T(1024)}, u32[]{:S(2)}) copy-start(f32[2048]{0:T(1024)} %param.27) | copy-start | bytes 24580
  3160.1 326.1 %copy-start.52 = (f32[2,192]{1,0:T(2,128)S(1)}, f32[2,192]{1,0:T(2,128)}, u32[]{:S(2)}) copy-start(f32[2,192]{1,0:T(2,128)} %copy-done.51) | copy-start | bytes 4612
  3486.2 51.5 %copy-start.54 = (f32[2,192]{1,0:T(2,128)S(1)}, f32[2,192]{1,0:T(2,128)}, u32[]{:S(2)}) copy-start(f32[2,192]{1,0:T(2,128)} %copy-done.53) | copy-start | bytes 4612
  3486.2 80.6 %copy-start.45 = (f32[2048]{0:T(1024)S(1)}, f32[2048]{0:T(1024)}, u32[]{:S(2)}) copy-start(f32[2048]{0:T(1024)} %param.28) | copy-start | bytes 24580
  3486.2 80.6 %copy-start.49 = (f32[2,192]{1,0:T(2,128)S(1)}, f32[2,192]{1,0:T(2,128)}, u32[]{:S(2)}) copy-start(f32[2,192]{1,0:T(2,128)} %copy-done.47) | copy-start | bytes 4612
  3486.3 80.6 %copy-start.58 = (f32[2,192]{1,0:T(2,128)S(1)}, f32[2,192]{1,0:T(2,128)}, u32[]{:S(2)}) copy-start(f32[2,192]{1,0:T(2,128)} %copy-done.57) | copy-start | bytes 4612
  3671.8 3.7 copy-start.27
  3671.8 5.2 copy-start.1
  (41 other events, 84.8 us)
Sparse Core Ops, SparseCore 0:
  12.8 47.6 all-gather.11
  62.8 45.1 all-gather.13
  110.2 88.1 all-gather.17
  200.4 87.8 all-gather.15
  290.2 46.6 all-gather.19
  448.3 75.4 reduce-scatter.19
  529.5 44.9 all-gather.21
  576.9 126.8 all-gather.25
  706.3 124.9 all-gather.23
  832.8 43.0 all-gather.29
  878.2 130.3 all-gather.27
  1085.1 75.2 reduce-scatter.23
  1167.4 44.9 all-gather.31
  1498.0 85.2 reduce-scatter.35
  2201.9 85.2 reduce-scatter.33
  2540.4 184.8 all-reduce.10
  2728.9 65.1 reduce-scatter.37
  2798.1 177.4 reduce-scatter.39
  2979.7 177.5 reduce-scatter.31
  3161.3 177.5 reduce-scatter.29
  3342.6 65.2 reduce-scatter.27
  3410.2 75.9 reduce-scatter.25
  3488.6 78.1 reduce-scatter.21
  3569.1 102.6 all-reduce.12
